TPU v7x, 32 devices: a whole 2x2x4 slice. The times are simulated.
32 devices in a mesh: row: 4 (over y, x), col: 8 (over z, core).
Axes of the slice: x: 2, y: 2, z: 4, core: 2. Of those that a mesh axis runs over, the one named last changes fastest.
Arguments:
- amplitudes: bfloat16 [16384, 16384], P('row', 'col'), may hold values from -6 to 6
- aux_left: bfloat16 [16384, 1024], P('col', 'row'), may hold values from -0.046875 to 0.046875
- aux_right: bfloat16 [16384, 1024], P('col', 'row'), may hold values from -0.1875 to 0.1875
- occupied_map: int32 [16384], replicated, may hold values from 0 to 63
- virtual_map: int32 [16384], replicated, may hold values from 0 to 255
- occupied_energy: float32 [64], replicated, may hold values from -3 to -0.5
- virtual_energy: float32 [256], replicated, may hold values from 0.5 to 4
Outputs:
- residual_term: float32 [16384, 16384], P('row', 'col')
All inputs are finite; a program needn't handle non-finite values.
Results may differ from a plain program's by a relative error of at most 0.0029.
Values may be sent and summed in bfloat16 or wider, within the bound.
A program may use at most 192 MiB of HBM per device.

v0:
```python
import jax
import jax.numpy as jnp
from jax import lax
from jax.sharding import PartitionSpec as P


def spread(shard, axis, root):
    mine = lax.axis_index(axis) == root
    return lax.psum(jnp.where(mine, shard, jnp.zeros_like(shard)), axis)


def lookup(positions, energy_table):
    matches = positions[:, None] == jnp.arange(energy_table.shape[0], dtype=jnp.int32)[None, :]
    return jnp.sum(jnp.where(matches, energy_table[None, :], 0.0), axis=1)


def pair_gap(occupied_map, virtual_map, occupied_energy, virtual_energy, offset, length):
    occupied_part = lax.dynamic_slice_in_dim(occupied_map, offset, length, 0)
    virtual_part = lax.dynamic_slice_in_dim(virtual_map, offset, length, 0)
    return lookup(virtual_part, virtual_energy) - lookup(occupied_part, occupied_energy)


def per_device(
    amplitudes, aux_left, aux_right, occupied_map, virtual_map, occupied_energy, virtual_energy
):
    rows_here, cols_here = amplitudes.shape
    fold_count = lax.axis_size("col") // lax.axis_size("row")
    row_block = lax.axis_index("row")
    col_block = lax.axis_index("col")
    partial_fitted = jnp.dot(
        amplitudes,
        lax.all_gather(aux_left, "row", axis=1, tiled=True),
        preferred_element_type=jnp.float32,
    )
    fitted_share = lax.psum_scatter(partial_fitted, "col", scatter_dimension=1, tiled=True).astype(
        jnp.bfloat16
    )
    fitted = lax.all_gather(fitted_share, "col", axis=1, tiled=True)
    right_block = lax.all_gather(aux_right, "row", axis=1, tiled=True)
    mixed = lax.dot_general(
        fitted, right_block, (((1,), (1,)), ((), ())), preferred_element_type=jnp.float32
    )
    mirror_slab = lax.dynamic_slice_in_dim(fitted, col_block % fold_count * cols_here, cols_here, 0)
    fitted_mirror = spread(mirror_slab, "row", col_block // fold_count)
    mirror_parts = []
    for member in range(fold_count):
        owned_rows = spread(right_block, "col", row_block * fold_count + member)
        mirror_parts.append(
            lax.dot_general(
                owned_rows,
                fitted_mirror,
                (((1,), (1,)), ((), ())),
                preferred_element_type=jnp.float32,
            )
        )
    mirrored = jnp.concatenate(mirror_parts, axis=0)
    row_gap = pair_gap(
        occupied_map, virtual_map, occupied_energy, virtual_energy, row_block * rows_here, rows_here
    )
    col_gap = pair_gap(
        occupied_map, virtual_map, occupied_energy, virtual_energy, col_block * cols_here, cols_here
    )
    denominator = row_gap[:, None] + col_gap[None, :]
    return (mixed + mirrored) / denominator


def solution(mesh):
    return jax.shard_map(
        per_device,
        mesh=mesh,
        in_specs=(P("row", "col"), P("col", "row"), P("col", "row"), P(), P(), P(), P()),
        out_specs=P("row", "col"),
        check_vma=False,
    )
```

profile of v0, /device:TPU:0, one launch (start us, length us, event | category | flops | bytes accessed | tf_op | source)
XLA Modules:
  0.0 744.1 jit_solution(4930799002853313942)
XLA Ops:
  6.5 0.0 all-gather.4.cloned.1.call-start
  6.5 0.7 all-gather.4.cloned.1.call-update
  7.3 0.0 reduce-scatter.2.cloned.1.call-start
  7.3 57.2 %all-gather.4.cloned.1.call-done = bf16[2048,1024]{1,0:T(8,128)(2,1)} async-done(((bf16[2048,256]{1,0:T(8,128)(2,1)}), bf16[2048,1024]{1,0:T(8,128)(2,1)}) %all-gather.4.cloned.1.call-update) | async-done | bytes 4194320 | tf_op jit(solution)/shard_map/all_gather | solution.py:32
  64.5 23.5 %fusion.1 = f32[4096,1024]{1,0:T(8,128)} fusion(bf16[4096,2048]{1,0:T(8,128)(2,1)} %param.7, bf16[2048,1024]{1,0:T(8,128)(2,1)} %all-gather.4.cloned.1.call-done), kind=kOutput, calls=%fused_computation.13 | convolution fusion | flops 17179869184 | bytes 37748736 | tf_op jit(solution)/shard_map/dot_general | solution.py:30
  87.9 0.0 reduce-scatter.2.cloned.1.call-update
  88.0 0.0 all-gather.8.cloned.1.call-start
  88.0 0.7 all-gather.8.cloned.1.call-update
  88.7 0.0 all-gather.6.cloned.1.call-start
  88.7 167.6 %reduce-scatter.2.cloned.1.call-done = f32[4096,128]{1,0:T(8,128)} async-done(((f32[4096,1024]{1,0:T(8,128)}), f32[4096,128]{1,0:T(8,128)}) %reduce-scatter.2.cloned.1.call-update) | async-done | bytes 2097168 | tf_op jit(solution)/shard_map/reduce_scatter | solution.py:35
  256.4 2.7 convert_element_type.3
  259.1 0.0 all-gather.6.cloned.1.call-update
  259.1 0.0 all-reduce.6.cloned.1.call-start
  259.2 50.0 %all-gather.8.cloned.1.call-done = bf16[2048,1024]{1,0:T(8,128)(2,1)} async-done(((bf16[2048,256]{1,0:T(8,128)(2,1)}), bf16[2048,1024]{1,0:T(8,128)(2,1)}) %all-gather.8.cloned.1.call-update) | async-done | bytes 4194320 | tf_op jit(solution)/shard_map/all_gather | solution.py:39
  309.2 6.0 broadcast_select_fusion.1
  315.2 0.0 all-reduce.6.cloned.1.call-update
  315.2 0.2 all-reduce.4.cloned.1.call-start
  315.5 77.7 %all-gather.6.cloned.1.call-done = bf16[4096,1024]{1,0:T(8,128)(2,1)} async-done(((bf16[4096,128]{1,0:T(8,128)(2,1)}), bf16[4096,1024]{1,0:T(8,128)(2,1)}) %all-gather.6.cloned.1.call-update) | async-done | bytes 8388624 | tf_op jit(solution)/shard_map/all_gather | solution.py:38
  393.2 5.3 dynamic-slice_select_fusion
  398.5 0.0 copy-start.1
  398.5 0.0 copy-start
  398.5 0.0 all-reduce.4.cloned.1.call-update
  398.5 0.7 dynamic_slice.19
  399.3 0.7 dynamic_slice.18
  400.0 0.7 dynamic_slice.17
  400.7 0.7 dynamic_slice.16
  401.4 0.0 copy-done.1
  401.4 0.2 select_reduce_fusion.3
  401.6 0.0 copy-done
  401.6 0.7 select_reduce_fusion.1
  402.3 0.2 select_reduce_fusion.2
  402.6 1.3 select_reduce_fusion
  403.9 165.7 %all-reduce.6.cloned.1.call-done = (bf16[2048,1024]{1,0:T(8,128)(2,1)}, bf16[2048,1024]{1,0:T(8,128)(2,1)}) async-done(((bf16[2048,1024]{1,0:T(8,128)(2,1)}, bf16[2048,1024]{1,0:T(8,128)(2,1)}), (bf16[2048,1024]{1,0:T(8,128)(2,1)}, bf16[2048,1024]{1,0:T(8,128)(2,1)})) %all-reduce.6.cloned.1.call-update) | async-done | bytes 8388624 | tf_op jit(solution)/shard_map/psum | solution.py:9
  569.6 107.1 %all-reduce.4.cloned.1.call-done = bf16[2048,1024]{1,0:T(8,128)(2,1)} async-done(((bf16[2048,1024]{1,0:T(8,128)(2,1)}), bf16[2048,1024]{1,0:T(8,128)(2,1)}) %all-reduce.4.cloned.1.call-update) | async-done | bytes 4194320 | tf_op jit(solution)/shard_map/psum | solution.py:9
  676.7 0.0 copy-start.2
  676.7 0.0 copy-start.3
  676.7 15.4 %fusion.3 = f32[2048,2048]{1,0:T(8,128)} fusion(bf16[2048,1024]{1,0:T(8,128)(2,1)} %get-tuple-element.5, bf16[2048,1024]{1,0:T(8,128)(2,1)} %all-reduce.4.cloned.1.call-done), kind=kOutput, calls=%fused_computation.15 | convolution fusion | flops 8589934592 | bytes 25165824 | tf_op jit(solution)/shard_map/dot_general | solution.py:49
  692.1 0.0 copy-done.2
  692.1 0.0 copy-done.3
  692.1 11.7 %fusion.2 = f32[2048,2048]{1,0:T(8,128)} fusion(bf16[2048,1024]{1,0:T(8,128)(2,1)S(1)} %copy-done.2, bf16[2048,1024]{1,0:T(8,128)(2,1)S(1)} %copy-done.3), kind=kOutput, calls=%fused_computation.14 | convolution fusion | flops 8589934592 | bytes 25165824 | tf_op jit(solution)/shard_map/dot_general | solution.py:49
  703.8 33.4 %fusion = f32[4096,2048]{1,0:T(8,128)} fusion(f32[2048,2048]{1,0:T(8,128)} %fusion.3, f32[2048,2048]{1,0:T(8,128)} %fusion.2, bf16[4096,1024]{1,0:T(8,128)(2,1)} %all-gather.6.cloned.1.call-done, bf16[2048,1024]{1,0:T(8,128)(2,1)} %all-gather.8.cloned.1.call-done, f32[2048]{0:T(1024)S(1)} %sub.20, f32[4096]{0:T(1024)S(1)} %sub.19), kind=kOutput, calls=%fused_computation.1 | convolution fusion | flops 17213423616 | bytes 79716352 | tf_op jit(solution)/shard_map/dot_general | solution.py:40
  (2 shorter events, 0.0 us)
Async XLA Ops:
  6.5 57.9 %all-gather.4.cloned.1.call-start = ((), (), s32[]{:S(2)}) async-start(), calls=%async_computation.1 | async-start | bytes 5242880 | tf_op jit(solution)/shard_map/all_gather | solution.py:32
  7.3 249.1 %reduce-scatter.2.cloned.1.call-start = ((), (), s32[]{:S(2)}) async-start(), calls=%async_computation.2 | async-start | bytes 18874368 | tf_op jit(solution)/shard_map/reduce_scatter | solution.py:35
  88.0 221.2 %all-gather.8.cloned.1.call-start = ((), (), s32[]{:S(2)}) async-start(), calls=%async_computation.4 | async-start | bytes 5242880 | tf_op jit(solution)/shard_map/all_gather | solution.py:39
  88.7 304.5 %all-gather.6.cloned.1.call-start = ((), (), s32[]{:S(2)}) async-start(), calls=%async_computation.3 | async-start | bytes 9437184 | tf_op jit(solution)/shard_map/all_gather | solution.py:38
  259.1 310.5 %all-reduce.6.cloned.1.call-start = ((), (), s32[]{:S(2)}) async-start(), calls=%async_computation.6 | async-start | bytes 16777216 | tf_op jit(solution)/shard_map/psum | solution.py:9
  315.2 361.5 %all-reduce.4.cloned.1.call-start = ((), (), s32[]{:S(2)}) async-start(), calls=%async_computation.5 | async-start | bytes 8388608 | tf_op jit(solution)/shard_map/psum | solution.py:9
  398.5 2.9 copy-start.1
  398.5 3.1 copy-start
  676.7 15.4 %copy-start.2 = (bf16[2048,1024]{1,0:T(8,128)(2,1)S(1)}, bf16[2048,1024]{1,0:T(8,128)(2,1)}, u32[]{:S(2)}) copy-start(bf16[2048,1024]{1,0:T(8,128)(2,1)} %get-tuple-element.6) | copy-start | bytes 12582916
  676.7 15.4 %copy-start.3 = (bf16[2048,1024]{1,0:T(8,128)(2,1)S(1)}, bf16[2048,1024]{1,0:T(8,128)(2,1)}, u32[]{:S(2)}) copy-start(bf16[2048,1024]{1,0:T(8,128)(2,1)} %all-reduce.4.cloned.1.call-done) | copy-start | bytes 12582916
Sparse Core Ops, SparseCore 0:
  9.2 55.2 all-gather.3
  88.1 168.2 reduce-scatter.1
  258.2 50.9 all-gather.7
  310.6 82.4 all-gather.5
  395.4 174.1 all-reduce.5
  572.7 103.9 all-reduce.3
where the time goes:
time: 745 us; the launch traced here: 744 us
  waiting for transfers between devices  627 us (84%)
  matrix products  84 us (11%)
  other arithmetic  16.6 us (2%)
  between operations  13.6 us (2%)
    psum x2, waiting for transfers between devices, spread(): return lax.psum(jnp.where(mine, shard, jnp.zeros_like(shard)), axis)  273 us
    reduce_scatter x1, waiting for transfers between devices, per_device(): lax.psum_scatter(partial_fitted, 'col', scatter_dimension=1, tiled=True)  168 us
    all_gather x1, waiting for transfers between devices, per_device(): fitted = lax.all_gather(fitted_share, 'col', axis=1, tiled=True)  77.7 us
    all_gather x1, waiting for transfers between devices, per_device(): lax.all_gather(aux_left, 'row', axis=1, tiled=True)  57.2 us
    all_gather x1, waiting for transfers between devices, per_device(): right_block = lax.all_gather(aux_right, 'row', axis=1, tiled=True)  50 us
    dot_general x1, matrix products, per_device(): lax.dot_general(fitted, right_block, (((1,), (1,)), ((), ())), preferred_...  33.4 us
    dot_general x2, matrix products, per_device(): lax.dot_general(owned_rows, fitted_mirror, (((1,), (1,)), ((), ())), pref...  27.1 us
    dot_general x1, matrix products, per_device(): jnp.dot(amplitudes, lax.all_gather(aux_left, 'row', axis=1, tiled=True),...  23.5 us
  transfers between devices with their start and end apart: 6, of which 6 were waited for; matrix products, arithmetic and copies ran while one was open for 3% of the time, Pallas kernels for 0%

commit v1 on v0

v1 whole, which is shorter than its diff:
```python
import functools

import jax
import jax.numpy as jnp
from jax import lax
from jax.experimental import pallas as pl
from jax.experimental.pallas import tpu as pltpu
from jax.sharding import PartitionSpec as P

MESH = pl.DeviceIdType.MESH
SKEW = 2
HOP = 4
TILE = 128


def lookup(positions, energy_table):
    matches = positions[:, None] == jnp.arange(energy_table.shape[0], dtype=jnp.int32)[None, :]
    return jnp.sum(jnp.where(matches, energy_table[None, :], 0.0), axis=1)


def pair_gap(occupied_map, virtual_map, occupied_energy, virtual_energy, offset, length):
    occupied_part = lax.dynamic_slice_in_dim(occupied_map, offset, length, 0)
    virtual_part = lax.dynamic_slice_in_dim(virtual_map, offset, length, 0)
    return lookup(virtual_part, virtual_energy) - lookup(occupied_part, occupied_energy)


def gather_kernel(
    n_row, n_col, amp, left, right,
    fitted, mirror, right_cols, right_rows, line,
    amp_v, left_v, chain_v, pair_v, give_v, done_v,
    amp_sem, left_send, left_recv, rc_send, rc_recv,
    chain_send, chain_recv, pair_send, pair_recv,
    back_send, back_recv, done_sem, mir_send, mir_recv,
    line_send, line_recv, rr_send, rr_recv, half_send, half_recv,
    fit_send, fit_recv, own_sem,
):
    rows_here, cols_here = amp.shape
    fold = n_col // n_row
    folds = fold // 2
    n_z = n_col // 2
    tile = chain_v.shape[2]
    per_sub = cols_here // 2 // tile
    n_t = folds * per_sub
    n = n_row * n_t
    row = lax.axis_index("row")
    col = lax.axis_index("col")
    z = col // 2
    core = col % 2
    sib = {"col": col + 1 - 2 * core}
    owner = (col // fold) == row

    def remote(src, dst, send, recv, where):
        return pltpu.make_async_remote_copy(
            src_ref=src, dst_ref=dst, send_sem=send, recv_sem=recv,
            device_id=where, device_id_type=MESH,
        )

    def peer(b):
        return {"row": (row - b + n_row) % n_row}

    def start_row(m, d, t):
        return pl.multiple_of(
            (2 * (t // per_sub) + m) * cols_here + d * (cols_here // 2) + (t % per_sub) * tile, tile
        )

    barrier = pltpu.get_barrier_semaphore()
    pl.semaphore_signal(barrier, inc=1, device_id=sib, device_id_type=MESH)
    for b in range(1, n_row):
        pl.semaphore_signal(barrier, inc=1, device_id=peer(b), device_id_type=MESH)

    @pl.when(z > 0)
    def _():
        pl.semaphore_signal(barrier, inc=1, device_id={"col": col - 2}, device_id_type=MESH)

    @pl.when(z < n_z - 1)
    def _():
        pl.semaphore_signal(barrier, inc=1, device_id={"col": col + 2}, device_id_type=MESH)

    amp_copy = pltpu.make_async_copy(amp, amp_v, amp_sem)
    amp_copy.start()
    own_left = pltpu.make_async_copy(left, left_v.at[row], own_sem.at[0])
    own_left.start()
    own_rc = pltpu.make_async_copy(right, right_cols.at[row], own_sem.at[1])
    own_rc.start()
    own_line = pltpu.make_async_copy(right, line.at[z], own_sem.at[2])
    own_line.start()

    line_ends = (z + n_z - 1) // n_z + (2 * (n_z - 1) - z) // n_z
    pl.semaphore_wait(barrier, n_row + line_ends)

    def left_copy(b):
        return remote(left, left_v.at[row], left_send.at[b], left_recv.at[b], peer(b))

    def rc_copy(b):
        return remote(
            right, right_cols.at[row], rc_send.at[b], rc_recv.at[b], peer(b)
        )

    for b in range(1, n_row):
        left_copy(b).start()
    own_line.wait()
    own_left.wait()
    own_rc.wait()
    amp_copy.wait()

    def product(m, d, i):
        j = (row + i // n_t) % n_row
        rows = amp_v[pl.ds(start_row(m, d, i % n_t), tile), :]
        return jnp.dot(rows, left_v[j], preferred_element_type=jnp.float32)

    def place(d, i):
        j = (row + i // n_t) % n_row
        return (j, pl.ds(start_row(core, d, i % n_t), tile))

    def send_mirror(d, i, src):
        t = i % n_t
        j = (row + i // n_t) % n_row

        @pl.when(jnp.logical_and(owner, t // per_sub == (col % fold) // 2))
        def _():
            at = pl.multiple_of(d * (cols_here // 2) + (t % per_sub) * tile, tile)
            for b in range(1, n_row):
                remote(
                    src, mirror.at[j, pl.ds(at, tile)],
                    mir_send.at[b], mir_recv, peer(b),
                ).start()

    def back(d, i, src):
        block, rows = place(d, i)
        remote(
            src, fitted.at[block, rows], back_send.at[d], back_recv.at[d, i],
            {"col": col + (2 if d else -2)},
        ).start()

    def line_copy(way, h):
        block = z - h + 1 if way == 0 else z + h - 1
        return remote(
            line.at[block], line.at[block], line_send.at[way, h], line_recv.at[way, h],
            {"col": col + (2 if way == 0 else -2)},
        )

    def line_sends(way, h):
        if way == 0:
            return jnp.logical_and(z + 1 < n_z, z - h + 1 >= 0)
        return jnp.logical_and(z >= 1, z + h - 1 < n_z)

    def line_gets(way, h):
        return z - h >= 0 if way == 0 else z + h < n_z

    def spread_rows(block, _):
        block_col = 2 * block + core
        dest = block_col // fold
        at = pl.multiple_of((block_col % fold) * cols_here, cols_here)
        target = right_rows.at[row, pl.ds(at, cols_here)]
        part = (block_col % fold) // 2

        @pl.when(dest == row)
        def _():
            pltpu.make_async_copy(line.at[block], target, rr_send.at[block]).start()

        @pl.when(dest != row)
        def _():
            remote(
                line.at[block], target, rr_send.at[block], rr_recv.at[row * folds + part],
                {"row": dest},
            ).start()

        return 0

    def step(s, _):
        for b in range(1, n_row):

            @pl.when(s == b * n_t - 1)
            def _():
                left_copy(b).wait_recv()
                rc_copy(b).start()

        @pl.when(s % HOP == 0)
        def _():
            h = s // HOP

            @pl.when(jnp.logical_and(h >= 1, h < n_z))
            def _():
                for way in (0, 1):

                    @pl.when(line_gets(way, h))
                    def _():
                        line_copy(way, h).wait_recv()

            @pl.when(h + 1 < n_z)
            def _():
                for way in (0, 1):

                    @pl.when(line_sends(way, h + 1))
                    def _():
                        line_copy(way, h + 1).start()

            @pl.when(h == n_z)
            def _():
                lax.fori_loop(0, n_z, spread_rows, 0)

        for d in (0, 1):
            depth = z if d == 0 else n_z - 1 - z
            i = s - 1 - SKEW * depth

            @pl.when(jnp.logical_and(i + 1 >= 0, i + 1 < n))
            def _():
                k = i + 1
                give_v[d, k] = product(1 - core, d, k)
                remote(
                    give_v.at[d, k], pair_v.at[d, k], pair_send.at[d], pair_recv.at[d, k], sib
                ).start()

            @pl.when(jnp.logical_and(i >= 0, i < n))
            def _():
                mine = product(core, d, i)
                remote(
                    give_v.at[d, i], pair_v.at[d, i], pair_send.at[d], pair_recv.at[d, i], sib
                ).wait_recv()
                pair_v[d, i] = mine + pair_v[d, i]

                def onward():
                    return remote(
                        chain_v.at[d, i], chain_v.at[d, i], chain_send.at[d],
                        chain_recv.at[d, i], {"col": col + (-2 if d else 2)},
                    )

                @pl.when(depth == 0)
                def _():
                    chain_v[d, i] = pair_v[d, i]

                @pl.when(depth > 0)
                def _():
                    onward().wait_recv()
                    chain_v[d, i] = chain_v[d, i] + pair_v[d, i]

                @pl.when(depth < n_z - 1)
                def _():
                    onward().start()

                @pl.when(depth == n_z - 1)
                def _():
                    done_v[d, i] = chain_v[d, i].astype(done_v.dtype)
                    block, rows = place(d, i)
                    pltpu.make_async_copy(
                        done_v.at[d, i], fitted.at[block, rows], done_sem.at[d]
                    ).start()
                    back(d, i, done_v.at[d, i])
                    send_mirror(d, i, done_v.at[d, i])

            away = n_z - 1 - depth
            g = s - 1 - SKEW * (n_z - 1) - SKEW * away

            @pl.when(jnp.logical_and(away > 0, jnp.logical_and(g >= 0, g < n)))
            def _():
                block, rows = place(d, g)
                here = fitted.at[block, rows]
                remote(
                    here, here, back_send.at[d], back_recv.at[d, g], sib
                ).wait_recv()

                @pl.when(away < n_z - 1)
                def _():
                    back(d, g, here)

                send_mirror(d, g, here)

        return 0

    lax.fori_loop(0, n + 1 + 2 * SKEW * (n_z - 1), step, 0)

    def rr_wait(block, _):
        remote(
            line.at[block], line.at[block], rr_send.at[block], rr_recv.at[0], sib
        ).wait_send()
        return 0

    lax.fori_loop(0, n_z, rr_wait, 0)

    def rr_got(k, _):
        @pl.when(k // folds != row)
        def _():
            remote(line.at[0], line.at[0], rr_send.at[0], rr_recv.at[k], sib).wait_recv()

        return 0

    lax.fori_loop(0, n_row * folds, rr_got, 0)

    for d in (0, 1):
        depth = z if d == 0 else n_z - 1 - z

        @pl.when(depth == n_z - 1)
        def _():
            pltpu.make_async_copy(done_v.at[d], done_v.at[d], done_sem.at[d]).wait()

    def half(ref, u, send, recv):
        at = pl.multiple_of((2 * u + core) * cols_here, cols_here)
        part = ref.at[:, pl.ds(at, cols_here)]
        return remote(part, part, send.at[u], recv.at[u], sib)

    for u in range(folds):
        half(right_rows, u, half_send, half_recv).start()
        half(fitted, u, fit_send, fit_recv).start()

    @pl.when(owner)
    def _():
        at = pl.multiple_of((col % fold) * cols_here, cols_here)
        own = pltpu.make_async_copy(fitted.at[:, pl.ds(at, cols_here)], mirror, own_sem.at[3])
        own.start()
        for b in range(1, n_row):
            remote(mirror, mirror, mir_send.at[b], mir_recv, sib).wait_send()
        own.wait()

    @pl.when(jnp.logical_not(owner))
    def _():
        remote(mirror, mirror, mir_send.at[0], mir_recv, sib).wait_recv()

    for u in range(folds):
        half(right_rows, u, half_send, half_recv).wait()
        half(fitted, u, fit_send, fit_recv).wait()
    for b in range(1, n_row):
        left_copy(b).wait_send()
        rc_copy(b).wait()

    def line_wait(h, _):
        for way in (0, 1):

            @pl.when(line_sends(way, h))
            def _():
                line_copy(way, h).wait_send()

        return 0

    lax.fori_loop(1, n_z, line_wait, 0)
    for d in (0, 1):
        depth = z if d == 0 else n_z - 1 - z
        remote(
            give_v.at[d], pair_v.at[d], pair_send.at[d], pair_recv.at[d, 0], sib
        ).wait_send()

        @pl.when(depth < n_z - 1)
        def _():
            remote(
                chain_v.at[d], chain_v.at[d], chain_send.at[d], chain_recv.at[d, 0], sib
            ).wait_send()

        @pl.when(depth > 0)
        def _():
            remote(
                done_v.at[d], done_v.at[d], back_send.at[d], back_recv.at[d, 0], sib
            ).wait_send()


def gather_all(amplitudes, aux_left, aux_right):
    n_row, n_col = lax.axis_size("row"), lax.axis_size("col")
    rows_here, cols_here = amplitudes.shape
    aux_block = aux_left.shape[1]
    aux = aux_block * n_row
    folds = n_col // n_row // 2
    n_z = n_col // 2
    tile = min(TILE, cols_here // 2)
    n = n_row * (rows_here // 4 // tile)
    dma = pltpu.SemaphoreType.DMA
    anywhere = pl.BlockSpec(memory_space=pl.ANY)
    low = amplitudes.dtype
    shapes = [
        (n_row, rows_here, aux_block), (n_row, cols_here, aux_block),
        (n_row, cols_here, aux_block), (n_row, rows_here, aux_block),
        (n_z, cols_here, aux_block),
    ]
    return pl.pallas_call(
        functools.partial(gather_kernel, n_row, n_col),
        out_shape=[jax.ShapeDtypeStruct(s, low) for s in shapes],
        in_specs=[anywhere] * 3,
        out_specs=[anywhere] * 5,
        scratch_shapes=[
            pltpu.VMEM((rows_here, cols_here), low),
            pltpu.VMEM((n_row, cols_here, aux_block), low),
            pltpu.VMEM((2, n, tile, aux_block), jnp.float32),
            pltpu.VMEM((2, n, tile, aux_block), jnp.float32),
            pltpu.VMEM((2, n, tile, aux_block), jnp.float32),
            pltpu.VMEM((2, n, tile, aux_block), low),
            dma(()), dma((n_row,)), dma((n_row,)), dma((n_row,)), dma((n_row,)),
            dma((2,)), dma((2, n)), dma((2,)), dma((2, n)),
            dma((2,)), dma((2, n)), dma((2,)), dma((n_row,)), dma(()),
            dma((2, n_z)), dma((2, n_z)), dma((n_z,)), dma((n_row * folds,)),
            dma((folds,)), dma((folds,)), dma((folds,)), dma((folds,)), dma((4,)),
        ],
        compiler_params=pltpu.CompilerParams(
            collective_id=0, has_side_effects=True, vmem_limit_bytes=58 * 2**20
        ),
        cost_estimate=pl.CostEstimate(
            flops=2 * rows_here * cols_here * aux, bytes_accessed=2 * rows_here * cols_here,
            transcendentals=0,
        ),
        name="gather_all",
    )(amplitudes, aux_left, aux_right)


def finish_kernel(fitted, right_rows, right_cols, mirror, row_gap, col_gap, out, held):
    blocks = range(fitted.shape[0])

    @pl.when(pl.program_id(0) == 0)
    def _():
        held[...] = jnp.concatenate(
            [right_cols[j] for j in blocks] + [mirror[j] for j in blocks], axis=1
        )

    rows = jnp.concatenate([fitted[j] for j in blocks] + [right_rows[j] for j in blocks], axis=1)
    total = lax.dot_general(
        rows, held[...], (((1,), (1,)), ((), ())), preferred_element_type=jnp.float32
    )
    out[...] = total / (row_gap[...] + col_gap[...])


def finish(fitted, right_rows, right_cols, mirror, row_gap, col_gap):
    n_row, rows_here, aux_block = fitted.shape
    cols_here = mirror.shape[1]
    tile = min(256, rows_here)
    by_row = pl.BlockSpec((n_row, tile, aux_block), lambda i: (0, i, 0))
    whole = pl.BlockSpec((n_row, cols_here, aux_block), lambda i: (0, 0, 0))
    return pl.pallas_call(
        finish_kernel,
        grid=(rows_here // tile,),
        out_shape=jax.ShapeDtypeStruct((rows_here, cols_here), jnp.float32),
        in_specs=[
            by_row, by_row, whole, whole,
            pl.BlockSpec((tile, 1), lambda i: (i, 0)),
            pl.BlockSpec((1, cols_here), lambda i: (0, 0)),
        ],
        out_specs=pl.BlockSpec((tile, cols_here), lambda i: (i, 0)),
        scratch_shapes=[pltpu.VMEM((cols_here, 2 * n_row * aux_block), fitted.dtype)],
        compiler_params=pltpu.CompilerParams(vmem_limit_bytes=52 * 2**20),
        name="finish",
    )(fitted, right_rows, right_cols, mirror, row_gap, col_gap)


def per_device(
    amplitudes, aux_left, aux_right, occupied_map, virtual_map, occupied_energy, virtual_energy
):
    rows_here, cols_here = amplitudes.shape
    gap = functools.partial(pair_gap, occupied_map, virtual_map, occupied_energy, virtual_energy)
    row_gap = gap(lax.axis_index("row") * rows_here, rows_here)
    col_gap = gap(lax.axis_index("col") * cols_here, cols_here)
    fitted, mirror, right_cols, right_rows, _ = gather_all(amplitudes, aux_left, aux_right)
    return finish(
        fitted, right_rows, right_cols, mirror, row_gap[:, None], col_gap[None, :]
    )


def solution(mesh):
    return jax.shard_map(
        per_device,
        mesh=mesh,
        in_specs=(P("row", "col"), P("col", "row"), P("col", "row"), P(), P(), P(), P()),
        out_specs=P("row", "col"),
        check_vma=False,
    )
```

time: 745 us -> 467 us (0.63)
  waiting for transfers between devices: 627 us -> 0 us
  Pallas kernels: 0 us -> 457 us
  matrix products: 84 us -> 0 us
  between operations: 13.6 us -> 0.05 us
  other arithmetic: 16.6 us -> 5.07 us
    pallas_call x0 -> x2, Pallas kernels: none -> 457 us  [the longest x1 412 us: gather_all(): pl.pallas_call(functools.partial(gather_kernel, n_row, n_col), out_shape=...]
    psum x2 -> x0, waiting for transfers between devices: 273 us -> none  [spread(): return lax.psum(jnp.where(mine, shard, jnp.zeros_like(shard)), axis)]
    all_gather x3 -> x0, waiting for transfers between devices: 185 us -> none  [the longest x1 77.7 us: per_device(): fitted = lax.all_gather(fitted_share, 'col', axis=1, tiled=True)]
    reduce_scatter x1 -> x0, waiting for transfers between devices: 168 us -> none  [per_device(): lax.psum_scatter(partial_fitted, 'col', scatter_dimension=1, tiled=True)]
    dot_general x4 -> x0, matrix products: 84 us -> none  [the longest x1 33.4 us: per_device(): lax.dot_general(fitted, right_block, (((1,), (1,)), ((), ())), preferred_...]
    select_n x2 -> x0, other arithmetic: 11.4 us -> none  [spread(): return lax.psum(jnp.where(mine, shard, jnp.zeros_like(shard)), axis)]
  transfers between devices with their start and end apart: 6 -> 0, of which waited for: 6 -> 0; matrix products, arithmetic and copies ran while one was open for 3% -> 0% of each run, Pallas kernels for 0% -> 0%
where the time goes in v1:
time: 467 us
  Pallas kernels  457 us (98%)
  other arithmetic  5.07 us (1%)
  local copies, waits for them, and re-layouts  4.86 us (1%)
    pallas_call x1, Pallas kernels, gather_all(): pl.pallas_call(functools.partial(gather_kernel, n_row, n_col), out_shape=...  412 us
    pallas_call x1, Pallas kernels, finish(): pl.pallas_call(finish_kernel, grid=(rows_here // tile,), out_shape=jax.Sh...  44.3 us

profile of v1, /device:TPU:0, one launch (start us, length us, event | category | flops | bytes accessed | tf_op | source)
XLA Modules:
  0.0 466.6 jit_solution(9397193916916099222)
XLA Ops:
  0.0 0.7 dynamic_slice.15
  0.7 0.8 select_reduce_fusion.3
  1.5 0.7 dynamic_slice.14
  2.2 1.4 select_reduce_fusion.1
  3.6 0.7 dynamic_slice.13
  4.4 0.9 select_reduce_fusion.2
  5.3 0.7 dynamic_slice.12
  6.0 1.9 select_reduce_fusion
  8.0 2.0 copy.9.row_gap
  10.0 412.3 %gather_all.1 = (bf16[4,4096,256]{2,1,0:T(8,128)(2,1)}, bf16[4,2048,256]{2,1,0:T(8,128)(2,1)}, bf16[4,2048,256]{2,1,0:T(8,128)(2,1)}, bf16[4,4096,256]{2,1,0:T(8,128)(2,1)}, bf16[4,2048,256]{2,1,0:T(8,128)(2,1)}) custom-call(bf16[4096,2048]{1,0:T(8,128)(2,1)} %amp.1, bf16[2048,256]{1,0:T(8,128)(2,1)} %left.1, bf16[2048,256]{1,0:T(8,128)(2,1)} %right.1), custom_call_target="tpu_custom_call" | custom-call | flops 17179869184 | bytes 16777216 | tf_op jit(solution)/shard_map/gather_all/pallas_call | solution.py:371
  422.3 44.3 %finish.1 = f32[4096,2048]{1,0:T(8,128)} custom-call(bf16[4,4096,256]{2,1,0:T(8,128)(2,1)} %get-tuple-element.9.fitted, bf16[4,4096,256]{2,1,0:T(8,128)(2,1)} %get-tuple-element.10.right_rows, bf16[4,2048,256]{2,1,0:T(8,128)(2,1)} %get-tuple-element.11.right_cols, bf16[4,2048,256]{2,1,0:T(8,128)(2,1)} %get-tuple-element.12.mirror, f32[4096,1]{1,0:T(8,128)} %copy.9.row_gap, ...), custom_call_target="tpu_custom_call" | custom-call | tf_op jit(solution)/shard_map/finish/pallas_call | solution.py:422
  (2 shorter events, 0.0 us)
